TPU v7x, 32 devices: a whole 2x2x4 slice. The times are simulated.
32 devices in a mesh: dp: 8 (over z, y), seq: 4 (over x, core).
Axes of the slice: x: 2, y: 2, z: 4, core: 2. Of those that a mesh axis runs over, the one named last changes fastest.
Arguments:
- tokens: bfloat16 [64, 512, 768], P('dp', 'seq'), may hold values from -8 to 8
- cotangent: bfloat16 [64, 512, 768], P('dp', 'seq'), may hold values from -6 to 6
- token_weight: float32 [64, 512], P('dp', 'seq'), may hold values from 0.25 to 2
- lengths: int32 [64], P('dp'), may hold values from 1 to 512, as said below
- qkv_master: float32 [768, 2304], P(('dp', 'seq')), may hold values from -1 to 1
- out_master: float32 [768, 768], P(('dp', 'seq')), may hold values from -0.625 to 0.625
- up_master: float32 [768, 3072], P(('dp', 'seq')), may hold values from -1 to 1
- down_master: float32 [3072, 768], P(('dp', 'seq')), may hold values from -0.109375 to 0.109375
- vec_master: float32 [9216], P(('dp', 'seq')), may hold values from -3 to 3
- qkv_first: float32 [768, 2304], P(('dp', 'seq')), may hold values from -0.00024414062 to 0.00024414062
- out_first: float32 [768, 768], P(('dp', 'seq')), may hold values from -0.00024414062 to 0.00024414062
- up_first: float32 [768, 3072], P(('dp', 'seq')), may hold values from -0.00024414062 to 0.00024414062
- down_first: float32 [3072, 768], P(('dp', 'seq')), may hold values from -0.00024414062 to 0.00024414062
- vec_first: float32 [9216], P(('dp', 'seq')), may hold values from -0.0007324219 to 0.0007324219
- qkv_second: float32 [768, 2304], P(('dp', 'seq')), may hold values from 7.0550676e-11 to 1.1288108e-09
- out_second: float32 [768, 768], P(('dp', 'seq')), may hold values from 7.0550676e-11 to 1.1288108e-09
- up_second: float32 [768, 3072], P(('dp', 'seq')), may hold values from 7.0550676e-11 to 1.1288108e-09
- down_second: float32 [3072, 768], P(('dp', 'seq')), may hold values from 7.0550676e-11 to 1.1288108e-09
- vec_second: float32 [9216], P(('dp', 'seq')), may hold values from 6.349561e-10 to 1.0159297e-08
Outputs:
- block_out: bfloat16 [64, 512, 768], P('dp', 'seq')
- input_grad: bfloat16 [64, 512, 768], P('dp', 'seq')
- grad_norm: float32 [], replicated
- qkv_new: float32 [768, 2304], P(('dp', 'seq'))
- qkv_first_new: float32 [768, 2304], P(('dp', 'seq'))
- qkv_second_new: float32 [768, 2304], P(('dp', 'seq'))
- qkv_copy: bfloat16 [768, 2304], P(('dp', 'seq'))
- out_new: float32 [768, 768], P(('dp', 'seq'))
- out_first_new: float32 [768, 768], P(('dp', 'seq'))
- out_second_new: float32 [768, 768], P(('dp', 'seq'))
- out_copy: bfloat16 [768, 768], P(('dp', 'seq'))
- up_new: float32 [768, 3072], P(('dp', 'seq'))
- up_first_new: float32 [768, 3072], P(('dp', 'seq'))
- up_second_new: float32 [768, 3072], P(('dp', 'seq'))
- up_copy: bfloat16 [768, 3072], P(('dp', 'seq'))
- down_new: float32 [3072, 768], P(('dp', 'seq'))
- down_first_new: float32 [3072, 768], P(('dp', 'seq'))
- down_second_new: float32 [3072, 768], P(('dp', 'seq'))
- down_copy: bfloat16 [3072, 768], P(('dp', 'seq'))
- vec_new: float32 [9216], P(('dp', 'seq'))
- vec_first_new: float32 [9216], P(('dp', 'seq'))
- vec_second_new: float32 [9216], P(('dp', 'seq'))
- vec_copy: bfloat16 [9216], P(('dp', 'seq'))
Inputs may be any that keep to these rules, and one draw needn't show every extreme that they name: Each index of dp holds 8 rows, and one of them, chosen at random, has length 512; the other lengths are mostly short.
All inputs are finite; a program needn't handle non-finite values.
Results may differ from a plain program's by a relative error of at most 0.012.
Values may be sent and summed in bfloat16 or wider, within the bound.
A program may use at most 192 MiB of HBM per device.

v0:
```python
import math

import jax
import jax.numpy as jnp
from jax import lax
from jax.sharding import PartitionSpec as P

D = 768
HEAD_DIM = 64
FF = 3072
STEP_COUNT = 10


CLIP_NORM = 1.0
BETA_ONE = 0.9
BETA_TWO = 0.999
LEARN_RATE = 0.05
VEC_RATE = 0.3
WEIGHT_DECAY = 0.01
ADAM_EPS = 1e-08
NORM_EPS = 1e-05
MASK_FILL = -1e30


def unpack(vector):
    return (
        vector[:D],
        vector[D : 2 * D],
        vector[2 * D : 3 * D],
        vector[3 * D : 4 * D],
        vector[4 * D : 5 * D],
        vector[5 * D : 5 * D + FF],
        vector[5 * D + FF : 6 * D + FF],
        vector[6 * D + FF : 7 * D + FF],
        vector[7 * D + FF : 8 * D + FF],
    )


def normalize(hidden, gain_vec, shift_vec):
    centre = hidden - jnp.mean(hidden, axis=-1, keepdims=True)
    inverse = lax.rsqrt(jnp.mean(centre * centre, axis=-1, keepdims=True) + NORM_EPS)
    normed = centre * inverse
    return (normed * gain_vec + shift_vec, normed, inverse)


def normalize_back(grad_out, normed, inverse, gain_vec):
    scaled = grad_out * gain_vec
    centred = scaled - jnp.mean(scaled, axis=-1, keepdims=True)
    return inverse * (centred - normed * jnp.mean(scaled * normed, axis=-1, keepdims=True))


def gelu_exact(values):
    return jax.nn.gelu(values, approximate=False)


def split_parts(packed_rows):
    full_len = packed_rows.shape[0]
    group_count = packed_rows.shape[-1] // HEAD_DIM
    parts = packed_rows.reshape(full_len, 3, group_count, HEAD_DIM)
    return (parts[:, 0], parts[:, 1], parts[:, 2])


def row_probs(queries, key_rows, key_mask):
    scale = 1.0 / math.sqrt(HEAD_DIM)
    scores = (
        jnp.einsum("qhd,khd->hqk", queries, key_rows, preferred_element_type=jnp.float32) * scale
    )
    scores = jnp.where(key_mask[None, None, :], scores, MASK_FILL)
    row_peak = jnp.max(scores, axis=-1, keepdims=True)
    row_exp = jnp.exp(scores - row_peak)
    return row_exp / jnp.sum(row_exp, axis=-1, keepdims=True)


def attend_row(packed):
    packed_rows, key_mask = packed
    queries, key_rows, value_rows = split_parts(packed_rows)
    attn_probs = row_probs(queries, key_rows, key_mask)
    mixed_rows = jnp.einsum(
        "hqk,khd->qhd",
        attn_probs.astype(jnp.bfloat16),
        value_rows,
        preferred_element_type=jnp.float32,
    )
    return mixed_rows.astype(jnp.bfloat16).reshape(packed_rows.shape[0], packed_rows.shape[-1])


def attend_back(packed):
    packed_rows, grad_rows, key_mask = packed
    full_len = packed_rows.shape[0]
    group_width = packed_rows.shape[-1]
    queries, key_rows, value_rows = split_parts(packed_rows)
    grad_mixed = grad_rows.reshape(full_len, group_width // HEAD_DIM, HEAD_DIM)
    attn_probs = row_probs(queries, key_rows, key_mask)
    grad_probs = jnp.einsum(
        "qhd,khd->hqk", grad_mixed, value_rows, preferred_element_type=jnp.float32
    )
    row_delta = jnp.sum(attn_probs * grad_probs, axis=-1, keepdims=True)
    grad_scores = (attn_probs * (grad_probs - row_delta)).astype(jnp.bfloat16)
    scale = 1.0 / math.sqrt(HEAD_DIM)
    grad_query = (
        jnp.einsum("hqk,khd->qhd", grad_scores, key_rows, preferred_element_type=jnp.float32)
        * scale
    )
    grad_key = (
        jnp.einsum("hqk,qhd->khd", grad_scores, queries, preferred_element_type=jnp.float32) * scale
    )
    grad_value = jnp.einsum(
        "hqk,qhd->khd",
        attn_probs.astype(jnp.bfloat16),
        grad_mixed,
        preferred_element_type=jnp.float32,
    )
    stacked = jnp.stack([grad_query, grad_key, grad_value], axis=1).astype(jnp.bfloat16)
    return stacked.reshape(full_len, 3, 1, group_width)


def adam_step(master, gradient, moment_one, second, factor, decay_rate, step_rate):
    clipped = gradient * factor
    first_new = BETA_ONE * moment_one + (1.0 - BETA_ONE) * clipped
    second_new = BETA_TWO * second + (1.0 - BETA_TWO) * clipped * clipped
    first_hat = first_new / (1.0 - BETA_ONE**STEP_COUNT)
    second_hat = second_new / (1.0 - BETA_TWO**STEP_COUNT)
    updated = master - step_rate * (
        first_hat / (jnp.sqrt(second_hat) + ADAM_EPS) + decay_rate * master
    )
    return (updated, first_new, second_new, updated.astype(jnp.bfloat16))


def body(
    tokens,
    cotangent,
    token_weight,
    lengths,
    qkv_master,
    out_master,
    up_master,
    down_master,
    vec_master,
    qkv_first,
    out_first,
    up_first,
    down_first,
    vec_first,
    qkv_second,
    out_second,
    up_second,
    down_second,
    vec_second,
):
    row_count, local_len, width_d = tokens.shape
    seq_count = lax.axis_size("seq")
    full_len = local_len * seq_count
    group_width = width_d // seq_count
    token_count = row_count * local_len
    qkv_w, out_w, up_w, down_w, vec_w = (
        lax.all_gather(qkv_master.astype(jnp.bfloat16), ("dp", "seq"), axis=0, tiled=True),
        lax.all_gather(out_master.astype(jnp.bfloat16), ("dp", "seq"), axis=0, tiled=True),
        lax.all_gather(up_master.astype(jnp.bfloat16), ("dp", "seq"), axis=0, tiled=True),
        lax.all_gather(down_master.astype(jnp.bfloat16), ("dp", "seq"), axis=0, tiled=True),
        lax.all_gather(vec_master.astype(jnp.bfloat16), ("dp", "seq"), axis=0, tiled=True),
    )
    bias_q, bias_v, bias_o, gain_one, shift_one, bias_up, bias_down, gain_two, shift_two = unpack(
        vec_w.astype(jnp.float32)
    )
    position = lax.axis_index("seq") * local_len + jnp.arange(local_len, dtype=jnp.int32)
    token_mask = (position[None, :] < lengths[:, None]).astype(jnp.float32)
    key_mask = jnp.arange(full_len, dtype=jnp.int32)[None, :] < lengths[:, None]
    flat_tokens = tokens.reshape(token_count, width_d)

    def project_heads():
        merged = jnp.dot(flat_tokens, qkv_w, preferred_element_type=jnp.float32)
        merged = merged + jnp.concatenate([bias_q, jnp.zeros_like(bias_q), bias_v])
        return merged.astype(jnp.bfloat16).reshape(row_count, local_len, 3, seq_count, group_width)

    heads_in = lax.all_to_all(project_heads(), "seq", split_axis=3, concat_axis=1, tiled=True)
    mixed_heads = lax.map(attend_row, (heads_in, key_mask))
    mixed_tok = lax.all_to_all(
        mixed_heads.reshape(row_count, full_len, 1, group_width),
        "seq",
        split_axis=1,
        concat_axis=2,
        tiled=True,
    )
    mixed_flat = mixed_tok.reshape(token_count, width_d)
    attn_out = jnp.dot(mixed_flat, out_w, preferred_element_type=jnp.float32) + bias_o
    first_out, normed_one, inverse_one = normalize(
        flat_tokens.astype(jnp.float32) + attn_out, gain_one, shift_one
    )
    first_low = first_out.astype(jnp.bfloat16)
    pre_act = jnp.dot(first_low, up_w, preferred_element_type=jnp.float32) + bias_up
    activated, gelu_pull = jax.vjp(gelu_exact, pre_act)
    act_low = activated.astype(jnp.bfloat16)
    branch = jnp.dot(act_low, down_w, preferred_element_type=jnp.float32) + bias_down
    result, normed_two, inverse_two = normalize(first_out + branch, gain_two, shift_two)
    block_out = result.astype(jnp.bfloat16).reshape(row_count, local_len, width_d)
    grad_result = (cotangent.astype(jnp.float32) * (token_weight * token_mask)[:, :, None]).reshape(
        token_count, width_d
    )
    grad_gain_two = jnp.sum(grad_result * normed_two, axis=0)
    grad_shift_two = jnp.sum(grad_result, axis=0)
    grad_second = normalize_back(grad_result, normed_two, inverse_two, gain_two)
    grad_branch = grad_second.astype(jnp.bfloat16)
    grad_bias_down = jnp.sum(grad_branch, axis=0, dtype=jnp.float32)
    grad_down = jnp.einsum("tf,td->fd", act_low, grad_branch, preferred_element_type=jnp.float32)
    grad_act = jnp.einsum("td,fd->tf", grad_branch, down_w, preferred_element_type=jnp.float32)
    grad_pre = gelu_pull(grad_act)[0].astype(jnp.bfloat16)
    grad_bias_up = jnp.sum(grad_pre, axis=0, dtype=jnp.float32)
    grad_up = jnp.einsum("td,tf->df", first_low, grad_pre, preferred_element_type=jnp.float32)
    grad_first = grad_second + jnp.einsum(
        "tf,df->td", grad_pre, up_w, preferred_element_type=jnp.float32
    )
    grad_gain_one = jnp.sum(grad_first * normed_one, axis=0)
    grad_shift_one = jnp.sum(grad_first, axis=0)
    grad_resid = normalize_back(grad_first, normed_one, inverse_one, gain_one)
    grad_attn = grad_resid.astype(jnp.bfloat16)
    grad_bias_o = jnp.sum(grad_attn, axis=0, dtype=jnp.float32)
    grad_out = jnp.einsum("td,te->de", mixed_flat, grad_attn, preferred_element_type=jnp.float32)
    grad_mixed = jnp.einsum(
        "te,de->td", grad_attn, out_w, preferred_element_type=jnp.float32
    ).astype(jnp.bfloat16)
    grad_heads = lax.all_to_all(
        grad_mixed.reshape(row_count, local_len, seq_count, group_width),
        "seq",
        split_axis=2,
        concat_axis=1,
        tiled=True,
    )
    heads_back = lax.all_to_all(project_heads(), "seq", split_axis=3, concat_axis=1, tiled=True)
    grad_block = lax.map(attend_back, (heads_back, grad_heads, key_mask))
    grad_tok = lax.all_to_all(grad_block, "seq", split_axis=1, concat_axis=3, tiled=True)
    grad_merged = grad_tok.reshape(token_count, 3 * width_d)
    grad_qkv = jnp.einsum("td,te->de", flat_tokens, grad_merged, preferred_element_type=jnp.float32)
    column_sums = jnp.sum(grad_merged, axis=0, dtype=jnp.float32)
    input_grad = grad_resid + jnp.einsum(
        "te,de->td", grad_merged, qkv_w, preferred_element_type=jnp.float32
    )
    input_grad = input_grad.astype(jnp.bfloat16).reshape(row_count, local_len, width_d)
    grad_vec = jnp.concatenate(
        [
            column_sums[:width_d],
            column_sums[2 * width_d :],
            grad_bias_o,
            grad_gain_one,
            grad_shift_one,
            grad_bias_up,
            grad_bias_down,
            grad_gain_two,
            grad_shift_two,
        ]
    )
    shards = (
        lax.psum_scatter(grad_qkv, ("dp", "seq"), scatter_dimension=0, tiled=True),
        lax.psum_scatter(grad_out, ("dp", "seq"), scatter_dimension=0, tiled=True),
        lax.psum_scatter(grad_up, ("dp", "seq"), scatter_dimension=0, tiled=True),
        lax.psum_scatter(grad_down, ("dp", "seq"), scatter_dimension=0, tiled=True),
        lax.psum_scatter(grad_vec, ("dp", "seq"), scatter_dimension=0, tiled=True),
    )
    squares = (
        jnp.sum(shards[0] * shards[0])
        + jnp.sum(shards[1] * shards[1])
        + jnp.sum(shards[2] * shards[2])
    )
    squares = squares + jnp.sum(shards[3] * shards[3]) + jnp.sum(shards[4] * shards[4])
    total_sq = lax.psum(squares, ("dp", "seq"))
    norm_value = jnp.sqrt(total_sq)
    factor = CLIP_NORM / jnp.maximum(norm_value, CLIP_NORM)
    qkv_up = adam_step(
        qkv_master, shards[0], qkv_first, qkv_second, factor, WEIGHT_DECAY, LEARN_RATE
    )
    out_up = adam_step(
        out_master, shards[1], out_first, out_second, factor, WEIGHT_DECAY, LEARN_RATE
    )
    ffn_up = adam_step(up_master, shards[2], up_first, up_second, factor, WEIGHT_DECAY, LEARN_RATE)
    down_up = adam_step(
        down_master, shards[3], down_first, down_second, factor, WEIGHT_DECAY, LEARN_RATE
    )
    vec_up = adam_step(vec_master, shards[4], vec_first, vec_second, factor, 0.0, VEC_RATE)
    return (
        block_out,
        input_grad,
        norm_value,
        qkv_up[0],
        qkv_up[1],
        qkv_up[2],
        qkv_up[3],
        out_up[0],
        out_up[1],
        out_up[2],
        out_up[3],
        ffn_up[0],
        ffn_up[1],
        ffn_up[2],
        ffn_up[3],
        down_up[0],
        down_up[1],
        down_up[2],
        down_up[3],
        vec_up[0],
        vec_up[1],
        vec_up[2],
        vec_up[3],
    )


def solution(mesh):
    in_specs = (
        P("dp", "seq", None),
        P("dp", "seq", None),
        P("dp", "seq"),
        P("dp"),
        P(("dp", "seq"), None),
        P(("dp", "seq"), None),
        P(("dp", "seq"), None),
        P(("dp", "seq"), None),
        P(("dp", "seq")),
        P(("dp", "seq"), None),
        P(("dp", "seq"), None),
        P(("dp", "seq"), None),
        P(("dp", "seq"), None),
        P(("dp", "seq")),
        P(("dp", "seq"), None),
        P(("dp", "seq"), None),
        P(("dp", "seq"), None),
        P(("dp", "seq"), None),
        P(("dp", "seq")),
    )
    out_specs = (
        P("dp", "seq", None),
        P("dp", "seq", None),
        P(),
        P(("dp", "seq"), None),
        P(("dp", "seq"), None),
        P(("dp", "seq"), None),
        P(("dp", "seq"), None),
        P(("dp", "seq"), None),
        P(("dp", "seq"), None),
        P(("dp", "seq"), None),
        P(("dp", "seq"), None),
        P(("dp", "seq"), None),
        P(("dp", "seq"), None),
        P(("dp", "seq"), None),
        P(("dp", "seq"), None),
        P(("dp", "seq"), None),
        P(("dp", "seq"), None),
        P(("dp", "seq"), None),
        P(("dp", "seq"), None),
        P(("dp", "seq")),
        P(("dp", "seq")),
        P(("dp", "seq")),
        P(("dp", "seq")),
    )
    return jax.shard_map(body, mesh=mesh, in_specs=in_specs, out_specs=out_specs, check_vma=False)
```

profile of v0, /device:TPU:0, one launch (start us, length us, event | category | flops | bytes accessed | tf_op | source)
XLA Modules:
  0.0 950.3 jit_solution(6302930151767969131)
XLA Ops:
  9.7 42.2 %all-reduce = bf16[9216]{0:T(1024)(128)(2,1)S(1)} all-reduce(bf16[9216]{0:T(1024)(128)(2,1)S(1)} %dynamic-update-slice), channel_id=1, replica_groups=mesh['dp'=8,'seq'=4] {'dp','seq'}, use_global_device_ids=true, to_apply=%add | all-reduce | flops 9216 | bytes 36864
  52.6 21.8 %all-gather.5.cloned.1.call-done = bf16[768,2304]{1,0:T(8,128)(2,1)} async-done(((bf16[24,2304]{1,0:T(8,128)(2,1)}), bf16[768,2304]{1,0:T(8,128)(2,1)}) %all-gather.5.cloned.1.call-update) | async-done | bytes 3538960 | tf_op jit(solution)/shard_map/all_gather | solution.py:156
  74.4 8.5 add_convert_fusion.1
  82.9 12.8 %reshape.229 = bf16[8,128,3,4,192]{4,3,2,1,0:T(4,128)(2,1)} reshape(bf16[1024,2304]{1,0:T(8,128)(2,1)} %add_convert_fusion.1) | data formatting | bytes 9437184 | tf_op jit(solution)/shard_map/reshape | solution.py:173
  95.7 8.2 copy.199
  103.9 5.1 all-to-all-start
  111.1 55.1 %all-to-all-done = bf16[8,128,3,4,192]{1,0,4,2,3:T(8,128)(2,1)} async-done(((bf16[8,128,3,4,192]{1,0,4,2,3:T(8,128)(2,1)}), bf16[8,128,3,4,192]{1,0,4,2,3:T(8,128)(2,1)}, u32[]{:S(2)}, u32[]{:S(2)}) %all-to-all-start) | async-done | bytes 4718624 | tf_op jit(solution)/shard_map/all_to_all | solution.py:175
  166.3 8.2 copy.200
  174.5 8.1 all_to_all.56
  182.5 50.6 %while.20 = (s32[]{:T(128)}, bf16[8,512,192]{1,2,0:T(8,128)(2,1)S(1)}, bf16[8,512,3,1,192]{1,4,2,3,0:T(8,128)(2,1)}, pred[8,512]{1,0:T(8,128)(4,1)S(1)}, s32[]{:T(128)}) while((s32[]{:T(128)}, bf16[8,512,192]{1,2,0:T(8,128)(2,1)S(1)}, bf16[8,512,3,1,192]{1,4,2,3,0:T(8,128)(2,1)}, pred[8,512]{1,0:T(8,128)(4,1)S(1)}, s32[]{:T(128)}) %tuple.124), condition=%wide.region_3.4_spmd, body=%wide.region_0.3_spmd.sunk | while | flops 206144000 | bytes 8666697 | solution.py:176
  183.7 2.8 fusion.111
  190.0 2.9 fusion.111
  196.3 2.9 fusion.111
  202.7 2.9 fusion.111
  209.0 2.9 fusion.111
  215.3 2.9 fusion.111
  221.7 2.9 fusion.111
  228.0 2.9 fusion.111
  233.8 3.1 copy.202
  236.8 3.7 all-to-all-start.1
  241.7 4.3 fusion.50
  246.0 21.3 %all-to-all-done.1 = bf16[8,512,1,192]{3,0,2,1:T(8,128)(2,1)S(1)} async-done(((bf16[8,512,1,192]{3,0,2,1:T(8,128)(2,1)}), bf16[8,512,1,192]{3,0,2,1:T(8,128)(2,1)S(1)}, u32[]{:S(2)}, u32[]{:S(2)}) %all-to-all-start.1) | async-done | bytes 1572896 | tf_op jit(solution)/shard_map/all_to_all | solution.py:177
  267.3 3.2 copy.203
  270.5 3.9 fusion.80
  274.9 35.7 %multiply_convert_fusion.1 = (bf16[1024,3072]{1,0:T(8,128)(2,1)}, f32[1024,3072]{1,0:T(8,128)}, f32[1024,3072]{1,0:T(8,128)}) fusion(f32[3072]{0:T(1024)S(1)} %slice.81, bf16[768,3072]{1,0:T(8,128)(2,1)} %all-gather.9.cloned.1.call-done, f32[1024,768]{1,0:T(8,128)S(1)} %get-tuple-element.360, f32[768]{0:T(1024)S(1)} %get-tuple-element.355, ...), kind=kOutput, calls=%fused_computation.53 | convolution fusion | flops 5043388416 | bytes 39348224 | tf_op jit(solution)/shard_map/dot_general | solution.py:190
  310.6 8.8 fusion.81
  323.0 3.7 convert_reduce_fusion.2
  326.6 18.9 %convert_reduce_fusion = (f32[3072]{0:T(1024)S(1)}, bf16[1024,3072]{1,0:T(8,128)(2,1)}) fusion(f32[1024,3072]{1,0:T(8,128)} %get-tuple-element.340, bf16[3072,768]{1,0:T(8,128)(2,1)} %all-gather.11.cloned.1.call-done, f32[1024,768]{1,0:T(8,128)} %get-tuple-element.336, f32[1024,3072]{1,0:T(8,128)} %get-tuple-element.361, f32[3072]{0:T(1024)S(1)} %slice.81), kind=kOutput, calls=%fused_computation.51 | convolution fusion | flops 4886098944 | bytes 39346176 | tf_op jit(solution)/shard_map/td,fd->tf/dot_general | solution.py:205
  345.5 10.0 %multiply_reduce_fusion.1 = (f32[768]{0:T(1024)S(1)}, f32[1024]{0:T(1024)S(1)}, f32[1024]{0:T(1024)S(1)}, f32[768]{0:T(1024)S(1)}, f32[1024,768]{1,0:T(8,128)S(1)}) fusion(f32[1024,768]{1,0:T(8,128)S(1)} %get-tuple-element.360, f32[1024]{0:T(1024)S(1)} %add_rsqrt_fusion.1, f32[1024]{0:T(1024)S(1)} %broadcast_multiply_fusion.4, ...), kind=kOutput, calls=%fused_computation.79 | convolution fusion | flops 4839698432 | bytes 20472832 | tf_op jit(solution)/shard_map/tf,df->td/dot_general | solution.py:209
  361.3 10.8 %fusion.58 = f32[3072,768]{1,0:T(8,128)} fusion(bf16[1024,3072]{1,0:T(8,128)(2,1)} %get-tuple-element.339, f32[1024,768]{1,0:T(8,128)} %get-tuple-element.336), kind=kOutput, calls=%fused_computation.154 | convolution fusion | flops 4832624640 | bytes 18874368 | tf_op jit(solution)/shard_map/tf,td->fd/dot_general | solution.py:204
  372.1 4.9 convolution_convert_fusion
  379.6 3.0 copy.224
  382.6 4.4 all-to-all-start.2
  387.0 10.7 %fusion.61 = f32[768,3072]{1,0:T(8,128)} fusion(bf16[1024,3072]{1,0:T(8,128)(2,1)} %get-tuple-element.366, f32[1024,768]{1,0:T(8,128)S(1)} %get-tuple-element.360, f32[768]{0:T(1024)S(1)} %get-tuple-element.355, f32[768]{0:T(1024)S(1)} %get-tuple-element.354, f32[1024]{0:T(1024)S(1)} %add_rsqrt_fusion.1, f32[1024]{0:T(1024)S(1)} %broadcast_multiply_fusion.4), kind=kOutput, calls=%fused_computation.157 | convolution fusion | flops 4835770368 | bytes 18888704 | tf_op jit(solution)/shard_map/td,tf->df/dot_general | solution.py:208
  397.8 9.3 all-to-all-done.2
  412.0 82.7 %while.21 = (s32[]{:T(128)}, bf16[8,512,3,1,192]{1,4,3,2,0:T(8,128)(2,1)}, bf16[8,512,3,1,192]{1,4,2,3,0:T(8,128)(2,1)}, pred[8,512]{1,0:T(8,128)(4,1)S(1)}, bf16[8,512,1,192]{1,3,2,0:T(8,128)(2,1)}, /*index=5*/s32[]{:T(128)}) while((s32[]{:T(128)}, bf16[8,512,3,1,192]{1,4,3,2,0:T(8,128)(2,1)}, bf16[8,512,3,1,192]{1,4,2,3,0:T(8,128)(2,1)}, ...), condition=%wide.region_16.17_spmd, body=%wide.region_12.16_spmd.sunk | while | flops 515800064 | bytes 30709868 | solution.py:229
  494.7 9.3 copy.208
  504.0 98.5 %all_to_all.71 = bf16[8,512,3,1,192]{4,0,3,2,1:T(8,128)(2,1)} all-to-all(bf16[8,512,3,1,192]{4,0,3,2,1:T(8,128)(2,1)} %copy.208), channel_id=1, replica_groups=mesh['dp'=8,'seq'=4] {'seq'}, dimensions={1} | all-to-all | bytes 9437184 | tf_op jit(solution)/shard_map/all_to_all | solution.py:230
  602.5 8.6 copy.220
  611.1 5.5 copy.210
  618.8 5.8 convolution_bitcast_fusion
  624.6 8.3 copy.221
  634.5 4.5 convert_reduce_fusion.1
  639.6 39.3 %all-reduce.1 = f32[9216]{0:T(1024)S(1)} all-reduce(f32[9216]{0:T(1024)S(1)} %constant_dynamic-update-slice_fusion.1), channel_id=6, replica_groups=mesh['dp'=8,'seq'=4] {'dp','seq'}, use_global_device_ids=true, to_apply=%region_33.34.clone | all-reduce | flops 9216 | bytes 73728
  681.2 74.7 %reduce-scatter.9.cloned.1.call-done = f32[24,3072]{1,0:T(8,128)} async-done(((f32[768,3072]{1,0:T(8,128)}), f32[24,3072]{1,0:T(8,128)}) %reduce-scatter.9.cloned.1.call-update) | async-done | bytes 294928 | tf_op jit(solution)/shard_map/reduce_scatter | solution.py:254
  757.5 123.1 %reduce-scatter.13.cloned.1.call-done = f32[24,2304]{1,0:T(8,128)} async-done(((f32[768,2304]{1,0:T(8,128)}), f32[24,2304]{1,0:T(8,128)}) %reduce-scatter.13.cloned.1.call-update) | async-done | bytes 221200 | tf_op jit(solution)/shard_map/reduce_scatter | solution.py:252
  886.3 9.5 add_convert_fusion.2
  895.8 40.2 %psum.7 = f32[]{:T(128)} all-reduce(f32[]{:T(128)S(6)} %add.218), channel_id=1, replica_groups=mesh['dp'=8,'seq'=4] {'dp','seq'}, use_global_device_ids=true, to_apply=%region_35.36 | all-reduce | flops 1 | bytes 8 | tf_op jit(solution)/shard_map/psum | solution.py:264
  (278 shorter events, 149.7 us)
Async XLA Ops:
  7.2 67.2 %all-gather.5.cloned.1.call-start = ((), (), s32[]{:S(2)}) async-start(), calls=%async_computation.8 | async-start | bytes 3649536 | tf_op jit(solution)/shard_map/all_gather | solution.py:156
  103.9 5.1 copy-start.17
  103.9 6.4 copy-start.7
  103.9 7.1 copy-start.33
  103.9 62.3 %all-to-all-start = ((bf16[8,128,3,4,192]{1,0,4,2,3:T(8,128)(2,1)}), bf16[8,128,3,4,192]{1,0,4,2,3:T(8,128)(2,1)}, u32[]{:S(2)}, u32[]{:S(2)}) async-start(bf16[8,128,3,4,192]{1,0,4,2,3:T(8,128)(2,1)} %copy.199), calls=%async_computation | async-start | bytes 9437184 | tf_op jit(solution)/shard_map/all_to_all | solution.py:175
  109.0 161.5 %all-gather.7.cloned.1.call-start = ((), (), s32[]{:S(2)}) async-start(), calls=%async_computation.9 | async-start | bytes 1216512 | tf_op jit(solution)/shard_map/all_gather | solution.py:157
  109.8 165.1 %all-gather.9.cloned.1.call-start = ((), (), s32[]{:S(2)}) async-start(), calls=%async_computation.10 | async-start | bytes 4866048 | tf_op jit(solution)/shard_map/all_gather | solution.py:158
  233.8 6.9 copy-start.5
  236.8 4.8 copy-start.32
  236.8 30.5 %all-to-all-start.1 = ((bf16[8,512,1,192]{3,0,2,1:T(8,128)(2,1)}), bf16[8,512,1,192]{3,0,2,1:T(8,128)(2,1)S(1)}, u32[]{:S(2)}, u32[]{:S(2)}) async-start(bf16[8,512,1,192]{3,0,2,1:T(8,128)(2,1)} %bitcast.201), calls=%async_computation.1 | async-start | bytes 4194304 | tf_op jit(solution)/shard_map/all_to_all | solution.py:177
  240.6 70.0 %all-gather.11.cloned.1.call-start = ((), (), s32[]{:S(2)}) async-start(), calls=%async_computation.11 | async-start | bytes 4866048 | tf_op jit(solution)/shard_map/all_gather | solution.py:159
  241.3 391.7 %reduce-scatter.7.cloned.1.call-start = ((), (), s32[]{:S(2)}) async-start(), calls=%async_computation.12 | async-start | bytes 2433024 | tf_op jit(solution)/shard_map/reduce_scatter | solution.py:253
  319.5 1.9 copy-start.1
  321.3 1.6 copy-start.27
  355.6 2.8 copy-start.4
  356.7 1.6 copy-start.3
  361.2 318.3 %reduce-scatter.11.cloned.1.call-start = ((), (), s32[]{:S(2)}) async-start(), calls=%async_computation.14 | async-start | bytes 9732096 | tf_op jit(solution)/shard_map/reduce_scatter | solution.py:255
  382.6 24.5 %all-to-all-start.2 = ((bf16[8,128,4,192]{1,0,3,2:T(8,128)(2,1)}), bf16[8,128,4,192]{1,0,3,2:T(8,128)(2,1)}, u32[]{:S(2)}, u32[]{:S(2)}) async-start(bf16[8,128,4,192]{1,0,3,2:T(8,128)(2,1)} %bitcast.202), calls=%async_computation.2 | async-start | bytes 3145728 | tf_op jit(solution)/shard_map/all_to_all | solution.py:221
  387.0 368.9 %reduce-scatter.9.cloned.1.call-start = ((), (), s32[]{:S(2)}) async-start(), calls=%async_computation.13 | async-start | bytes 9732096 | tf_op jit(solution)/shard_map/reduce_scatter | solution.py:254
  397.8 482.9 %reduce-scatter.13.cloned.1.call-start = ((), (), s32[]{:S(2)}) async-start(), calls=%async_computation.15 | async-start | bytes 7299072 | tf_op jit(solution)/shard_map/reduce_scatter | solution.py:252
  407.1 4.8 copy-start.23
  480.7 1.1 copy-start
  491.1 1.1 copy-start
  611.1 7.7 copy-start.36
  616.6 2.2 copy-start.2
  632.9 6.6 copy-start.29
  633.0 6.6 copy-start.30
  633.0 6.6 copy-start.28
  678.9 78.7 %copy-start.26 = (f32[9216]{0:T(1024)}, f32[9216]{0:T(1024)S(1)}, u32[]{:S(2)}) copy-start(f32[9216]{0:T(1024)S(1)} %all-reduce.1) | copy-start | bytes 110596
  886.1 50.6 %copy-start.31 = (f32[288]{0:T(512)S(1)}, f32[288]{0:T(512)}, u32[]{:S(2)}) copy-start(f32[288]{0:T(512)} %param.31) | copy-start | bytes 3460
  886.1 50.6 %copy-start.34 = (f32[288]{0:T(512)S(1)}, f32[288]{0:T(512)}, u32[]{:S(2)}) copy-start(f32[288]{0:T(512)} %param.36) | copy-start | bytes 3460
  886.1 50.6 %copy-start.35 = (f32[288]{0:T(512)S(1)}, f32[288]{0:T(512)}, u32[]{:S(2)}) copy-start(f32[288]{0:T(512)} %param.41) | copy-start | bytes 3460
  886.2 52.0 %copy-start.6 = (f32[96,768]{1,0:T(8,128)S(1)}, f32[96,768]{1,0:T(8,128)}, u32[]{:S(2)}) copy-start(f32[96,768]{1,0:T(8,128)} %param.30) | copy-start | bytes 884740
  886.2 52.0 %copy-start.9 = (f32[96,768]{1,0:T(8,128)S(1)}, f32[96,768]{1,0:T(8,128)}, u32[]{:S(2)}) copy-start(f32[96,768]{1,0:T(8,128)} %reduce-scatter.11.cloned.1.call-done) | copy-start | bytes 884740
  886.2 52.0 %copy-start.13 = (f32[96,768]{1,0:T(8,128)S(1)}, f32[96,768]{1,0:T(8,128)}, u32[]{:S(2)}) copy-start(f32[96,768]{1,0:T(8,128)} %param.35) | copy-start | bytes 884740
  886.2 52.0 %copy-start.14 = (f32[96,768]{1,0:T(8,128)S(1)}, f32[96,768]{1,0:T(8,128)}, u32[]{:S(2)}) copy-start(f32[96,768]{1,0:T(8,128)} %param.40) | copy-start | bytes 884740
  886.2 53.1 %copy-start.8 = (f32[24,3072]{1,0:T(8,128)S(1)}, f32[24,3072]{1,0:T(8,128)}, u32[]{:S(2)}) copy-start(f32[24,3072]{1,0:T(8,128)} %param.29) | copy-start | bytes 884740
  886.2 53.1 %copy-start.10 = (f32[24,3072]{1,0:T(8,128)S(1)}, f32[24,3072]{1,0:T(8,128)}, u32[]{:S(2)}) copy-start(f32[24,3072]{1,0:T(8,128)} %reduce-scatter.9.cloned.1.call-done) | copy-start | bytes 884740
  886.2 53.1 %copy-start.15 = (f32[24,3072]{1,0:T(8,128)S(1)}, f32[24,3072]{1,0:T(8,128)}, u32[]{:S(2)}) copy-start(f32[24,3072]{1,0:T(8,128)} %param.34) | copy-start | bytes 884740
  886.2 53.0 %copy-start.16 = (f32[24,3072]{1,0:T(8,128)S(1)}, f32[24,3072]{1,0:T(8,128)}, u32[]{:S(2)}) copy-start(f32[24,3072]{1,0:T(8,128)} %param.39) | copy-start | bytes 884740
  895.7 44.7 %copy-start.18 = (f32[24,768]{1,0:T(8,128)S(1)}, f32[24,768]{1,0:T(8,128)}, u32[]{:S(2)}) copy-start(f32[24,768]{1,0:T(8,128)} %param.28) | copy-start | bytes 221188
  895.7 44.7 %copy-start.19 = (f32[24,768]{1,0:T(8,128)S(1)}, f32[24,768]{1,0:T(8,128)}, u32[]{:S(2)}) copy-start(f32[24,768]{1,0:T(8,128)} %reduce-scatter.7.cloned.1.call-done) | copy-start | bytes 221188
  895.7 44.7 %copy-start.24 = (f32[24,768]{1,0:T(8,128)S(1)}, f32[24,768]{1,0:T(8,128)}, u32[]{:S(2)}) copy-start(f32[24,768]{1,0:T(8,128)} %param.33) | copy-start | bytes 221188
  895.7 44.7 %copy-start.25 = (f32[24,768]{1,0:T(8,128)S(1)}, f32[24,768]{1,0:T(8,128)}, u32[]{:S(2)}) copy-start(f32[24,768]{1,0:T(8,128)} %param.38) | copy-start | bytes 221188
  895.8 45.4 %copy-start.11 = (f32[24,2304]{1,0:T(8,128)S(1)}, f32[24,2304]{1,0:T(8,128)}, u32[]{:S(2)}) copy-start(f32[24,2304]{1,0:T(8,128)} %param.27) | copy-start | bytes 663556
  895.8 45.4 %copy-start.12 = (f32[24,2304]{1,0:T(8,128)S(1)}, f32[24,2304]{1,0:T(8,128)}, u32[]{:S(2)}) copy-start(f32[24,2304]{1,0:T(8,128)} %reduce-scatter.13.cloned.1.call-done) | copy-start | bytes 663556
  895.8 45.4 %copy-start.20 = (f32[24,2304]{1,0:T(8,128)S(1)}, f32[24,2304]{1,0:T(8,128)}, u32[]{:S(2)}) copy-start(f32[24,2304]{1,0:T(8,128)} %param.32) | copy-start | bytes 663556
  895.8 45.4 %copy-start.21 = (f32[24,2304]{1,0:T(8,128)S(1)}, f32[24,2304]{1,0:T(8,128)}, u32[]{:S(2)}) copy-start(f32[24,2304]{1,0:T(8,128)} %param.37) | copy-start | bytes 663556
  (7 other events, 7.0 us)
Sparse Core Ops, SparseCore 0:
  11.5 62.8 all-gather.4
  113.3 56.4 all-gather.6
  173.3 62.6 all-gather.8
  244.6 63.9 all-gather.10
  361.3 98.0 reduce-scatter.6
  466.2 149.1 reduce-scatter.10
  621.3 134.5 reduce-scatter.8
  762.5 118.1 reduce-scatter.12
where the time goes:
time: 960 us; the launch traced here: 950 us
  waiting for transfers between devices  306 us (32%)
  blocking collectives  220 us (23%)
  matrix products  215 us (22%)
  local copies, waits for them, and re-layouts  129 us (13%)
  other arithmetic  46.1 us (5%)
  between operations  20.1 us (2%)
  starting transfers between devices  14.2 us (1%)
    reduce_scatter x1, waiting for transfers between devices, body(): lax.psum_scatter(grad_qkv, ('dp', 'seq'), scatter_dimension=0, tiled=True)  123 us
    all_to_all x1, blocking collectives, body(): lax.all_to_all(grad_block, 'seq', split_axis=1, concat_axis=3, tiled=True)  98.5 us
    unnamed x2, blocking collectives  81.5 us
    reduce_scatter x1, waiting for transfers between devices, body(): lax.psum_scatter(grad_up, ('dp', 'seq'), scatter_dimension=0, tiled=True)  74.7 us
    all_to_all x1, waiting for transfers between devices, body(): lax.all_to_all(project_heads(), 'seq', split_axis=3, concat_axis=1, tiled...  55.1 us
    sub x16, matrix products, row_probs(): row_exp = jnp.exp(scores - row_peak)  41.3 us
    psum x1, blocking collectives, body(): total_sq = lax.psum(squares, ('dp', 'seq'))  40.2 us
    dot_general x1, matrix products, body(): jnp.dot(first_low, up_w, preferred_element_type=jnp.float32) + bias_up  35.7 us
  transfers between devices with their start and end apart: 11, of which 6 were waited for; matrix products, arithmetic and copies ran while one was open for 29% of the time, Pallas kernels for 0%

commit v1 on v0

v1 whole, which is shorter than its diff:
```python
import functools
import math

import jax
import jax.numpy as jnp
from jax import lax
from jax.experimental import pallas as pl
from jax.experimental.pallas import tpu as pltpu
from jax.sharding import PartitionSpec as P

D = 768
HEADS = 12
HEAD_DIM = 64
FF = 3072
STEP_COUNT = 10
CLIP_NORM = 1.0
BETA_ONE = 0.9
BETA_TWO = 0.999
LEARN_RATE = 0.05
VEC_RATE = 0.3
WEIGHT_DECAY = 0.01
ADAM_EPS = 1e-08
NORM_EPS = 1e-05
MASK_FILL = -1e30
MESH = pl.DeviceIdType.MESH
F32 = jnp.float32
BF16 = jnp.bfloat16
VMEM_LIMIT = 60 << 20


class Place:
    def __init__(self):
        self.ndp, self.nsq = lax.axis_size("dp"), lax.axis_size("seq")
        self.dp, self.sq = lax.axis_index("dp"), lax.axis_index("seq")
        self.z, self.y = self.dp // 2, self.dp % 2
        self.x, self.c = self.sq // 2, self.sq % 2
        self.nz = self.ndp // 2
        self.core = (self.dp, self.x * 2 + 1 - self.c)
        self.across_x = (self.dp, (1 - self.x) * 2 + self.c)
        self.across_y = (self.z * 2 + 1 - self.y, self.sq)

    def along_z(self, k):
        return (self.z + k) % self.nz

    def at_z(self, z):
        return (z * 2 + self.y, self.sq)


def greet(targets):
    barrier = pltpu.get_barrier_semaphore()
    for target in targets:
        pl.semaphore_signal(barrier, inc=1, device_id=target, device_id_type=MESH)
    pl.semaphore_wait(barrier, len(targets))


class Sems:
    def __init__(self, send, recv, local):
        self.send, self.recv, self.local = send, recv, local
        self.n = self.m = 0

    def remote(self, src, dst, target):
        i = self.n
        self.n += 1
        return pltpu.make_async_remote_copy(
            src_ref=src,
            dst_ref=dst,
            send_sem=self.send.at[i],
            recv_sem=self.recv.at[i],
            device_id=target,
            device_id_type=MESH,
        )

    def here(self, src, dst):
        i = self.m
        self.m += 1
        return pltpu.make_async_copy(src, dst, self.local.at[i])


def begin(copies):
    for copy in copies:
        copy.start()


def finish(copies):
    for copy in copies:
        copy.wait()


class Gather:
    def __init__(self, place, sems, at, own, x_first):
        p = place
        whole = slice(None)
        mine = at(p.z, p.y, p.x)
        self.stages = [
            [sems.here(own, mine)]
            + [sems.remote(own, mine, p.at_z(p.along_z(k))) for k in range(1, p.nz)]
        ]
        line = at(whole, p.y, p.x)
        if x_first:
            plane, hops = at(whole, p.y, whole), (p.across_x, p.across_y)
        else:
            plane, hops = at(whole, whole, p.x), (p.across_y, p.across_x)
        everything = at(whole, whole, whole)
        self.stages.append([sems.remote(line, line, hops[0])])
        self.stages.append([sems.remote(plane, plane, hops[1])])
        self.stages.append([sems.remote(everything, everything, p.core)])


def pipeline(items):
    depth = len(items[0].stages)

    def step(t):
        for s in reversed(range(depth)):
            i = t - s
            if 0 <= i < len(items):
                if s:
                    finish(items[i].stages[s - 1])
                begin(items[i].stages[s])
        i = t - depth
        if 0 <= i < len(items):
            finish(items[i].stages[depth - 1])

    return [functools.partial(step, t) for t in range(len(items) + depth)]


def tokens_to_rows(place, sems, src, dst, here):
    p = place
    part, length = dst.shape[0], src.shape[1]
    spot = dst.at[:, pl.ds(p.sq * length, length)]
    copies = [sems.here(src.at[pl.ds(p.sq * part, part)], spot)]
    for k in range(1, p.nsq):
        to = (p.sq + k) % p.nsq
        copies.append(sems.remote(src.at[pl.ds(to * part, part)], spot, (p.dp, to)))
    return copies


def rows_to_tokens(place, sems, src, dst):
    p = place
    part, length = src.shape[0], dst.shape[1]
    spot = dst.at[pl.ds(p.sq * part, part)]
    copies = [sems.here(src.at[:, pl.ds(p.sq * length, length)], spot)]
    for k in range(1, p.nsq):
        to = (p.sq + k) % p.nsq
        copies.append(sems.remote(src.at[:, pl.ds(to * length, length)], spot, (p.dp, to)))
    return copies


PIECES = {
    "qkv": ((0, 640, True), (640, 512, False)),
    "out": ((0, 384, True),),
    "up": ((0, 768, True), (768, 768, False)),
}


def gather_kernel(
    tokens, cotangent, weight, qkv_m, out_m, up_m, down_m, vec_m,
    x_rows, cot_rows, weight_all, qkv_w, out_w, up_w, down_w, vec_w,
    qkv_f, out_f, up_f, down_f, qkv_b, out_b, up_b, down_b, send, recv, local,
):
    p = Place()
    greet([p.core, p.across_x, p.across_y, (p.dp, 3 - p.sq)] + [p.at_z(p.along_z(k)) for k in range(1, p.nz)])
    sems = Sems(send, recv, local)
    move_tokens = tokens_to_rows(p, sems, tokens, x_rows, True)
    move_cot = tokens_to_rows(p, sems, cotangent, cot_rows, True)
    spot = weight_all.at[p.sq]
    move_weight = [sems.here(weight, spot)] + [
        sems.remote(weight, spot, (p.dp, (p.sq + k) % p.nsq)) for k in range(1, p.nsq)
    ]
    masters = {"qkv": (qkv_m, qkv_f, qkv_b, qkv_w), "out": (out_m, out_f, out_b, out_w), "up": (up_m, up_f, up_b, up_w)}
    rows = qkv_m.shape[0]
    mine = pl.ds(p.c * rows, rows)
    halves = {}
    for name, (master, wide, _, _) in masters.items():
        half = wide.shape[1]
        halves[name] = [
            sems.here(master.at[:, pl.ds(p.c * half, half)], wide.at[mine]),
            sems.remote(master.at[:, pl.ds((1 - p.c) * half, half)], wide.at[mine], p.core),
        ]
    load_down = [sems.here(down_m, down_f)]
    items = {}
    for name, (_, wide, low, whole) in masters.items():
        half = wide.shape[1]
        for offset, width, x_first in PIECES[name]:

            def at(z, y, x, whole=whole, half=half, offset=offset, width=width):
                return whole.at[z, y, x, :, pl.ds(p.c * half + offset, width)]

            items[name, offset] = Gather(p, sems, at, low.at[:, pl.ds(offset, width)], x_first)
    items["vec"] = Gather(p, sems, lambda z, y, x: vec_w.at[z, y, x, p.c], vec_m, False)
    items["down"] = Gather(p, sems, lambda z, y, x: down_w.at[z, y, x, p.c], down_b, True)

    begin(halves["qkv"])
    begin(move_tokens)
    begin(halves["out"])
    begin(halves["up"])
    begin(load_down)
    begin(move_weight)
    for name, (_, wide, low, _) in masters.items():
        finish(halves[name])
        low[...] = wide[...].astype(BF16)
    finish(load_down)
    down_b[...] = down_f[...].astype(BF16)
    order = [("qkv", 0), ("qkv", 640), "vec", ("out", 0), ("up", 0), ("up", 768), "down"]
    steps = pipeline([items[key] for key in order])
    for t, step in enumerate(steps):
        step()
        if t == 4:
            begin(move_cot)
    finish(move_tokens + move_cot + move_weight)


def gather_weights(tokens, cotangent, weight, qkv_m, out_m, up_m, down_m, vec_m):
    ndp, nsq = lax.axis_size("dp"), lax.axis_size("seq")
    rows, length, width = tokens.shape
    part, full = rows // nsq, length * nsq
    chip, low = 2 * qkv_m.shape[0], down_m.shape[0]
    grid = (ndp // 2, 2, nsq // 2)
    any_space = pl.BlockSpec(memory_space=pl.ANY)
    shapes = [
        jax.ShapeDtypeStruct((part, full, width), BF16),
        jax.ShapeDtypeStruct((part, full, width), BF16),
        jax.ShapeDtypeStruct((nsq,) + weight.shape, F32),
    ]
    shapes += [jax.ShapeDtypeStruct(grid + (chip, m.shape[1]), BF16) for m in (qkv_m, out_m, up_m)]
    shapes += [
        jax.ShapeDtypeStruct(grid + (2, low, down_m.shape[1]), BF16),
        jax.ShapeDtypeStruct(grid + (2,) + vec_m.shape, F32),
    ]
    half = [m.shape[1] // 2 for m in (qkv_m, out_m, up_m)]
    return pl.pallas_call(
        gather_kernel,
        out_shape=shapes,
        in_specs=[any_space] * 8,
        out_specs=[any_space] * 8,
        scratch_shapes=[pltpu.VMEM((chip, h), F32) for h in half]
        + [pltpu.VMEM(down_m.shape, F32)]
        + [pltpu.VMEM((chip, h), BF16) for h in half]
        + [pltpu.VMEM(down_m.shape, BF16)]
        + [pltpu.SemaphoreType.DMA((64,)), pltpu.SemaphoreType.DMA((64,)), pltpu.SemaphoreType.DMA((24,))],
        compiler_params=pltpu.CompilerParams(
            collective_id=1, has_side_effects=True, vmem_limit_bytes=VMEM_LIMIT
        ),
    )(tokens, cotangent, weight, qkv_m, out_m, up_m, down_m, vec_m)


def add_into(total, extra, lead):
    count = math.prod(lead)

    def one(i, carry):
        spot = []
        for size in reversed(lead):
            spot.insert(0, i % size)
            i = i // size
        spot = tuple(spot)
        total[spot] = (total[spot].astype(F32) + extra[spot].astype(F32)).astype(total.dtype)
        return carry

    lax.fori_loop(0, count, one, 0)


class Scatter:
    def __init__(self, place, sems, at, bufs, x_first):
        p = place
        total, near, first, second, along, final = bufs
        nz = p.nz
        self.stages = [
            [
                sems.here(at(p.c), total),
                sems.remote(at(1 - p.c), near, p.core),
            ]
        ]
        if x_first:
            self.stages.append([sems.remote(total.at[:, :, 1 - p.x], first, p.across_x)])
            kept = total.at[:, :, p.x]
            self.stages.append([sems.remote(total.at[:, 1 - p.y, p.x], second, p.across_y)])
        else:
            self.stages.append([sems.remote(total.at[:, 1 - p.y], first, p.across_y)])
            kept = total.at[:, p.y]
            self.stages.append([sems.remote(total.at[:, p.y, 1 - p.x], second, p.across_x)])
        line = total.at[:, p.y, p.x]
        self.stages.append(
            [
                sems.remote(total.at[p.along_z(k), p.y, p.x], along.at[k - 1], p.at_z(p.along_z(k)))
                for k in range(1, nz)
            ]
        )

        def close():
            value = total[p.z, p.y, p.x].astype(F32)
            for k in range(1, nz):
                value = value + along[k - 1].astype(F32)
            final[...] = value

        self.after = [
            lambda: add_into(total, near, (nz, 2, 2)),
            lambda: add_into(kept, first, (nz, 2)),
            lambda: add_into(line, second, (nz,)),
            close,
        ]


def scatter_pipeline(items):
    depth = 4

    def step(t):
        for s in reversed(range(depth + 1)):
            i = t - s
            if 0 <= i < len(items):
                if s:
                    finish(items[i].stages[s - 1])
                    items[i].after[s - 1]()
                if s < depth:
                    begin(items[i].stages[s])

    return [functools.partial(step, t) for t in range(len(items) + depth)]


def scatter_scratch(block, nz, dtype):
    return [
        pltpu.VMEM((nz, 2, 2) + block, dtype),
        pltpu.VMEM((nz, 2, 2) + block, dtype),
        pltpu.VMEM((nz, 2) + block, dtype),
        pltpu.VMEM((nz,) + block, dtype),
        pltpu.VMEM((nz - 1,) + block, dtype),
        pltpu.VMEM(block, F32),
    ]


def scatter_kernel(
    block_rows, grad_rows, qkv_g, out_g, up_g, down_g, vec_g,
    block_out, input_grad, qkv_s, out_s, up_s, down_s, vec_s, norm,
    *scratch,
):
    send, recv, local, near_sum, far_sum = scratch[-5:]
    p = Place()
    greet(
        [(p.dp, (p.sq + k) % p.nsq) for k in range(1, p.nsq)]
        + [((p.dp + k) % p.ndp, p.sq) for k in range(1, p.ndp)]
    )
    sems = Sems(send, recv, local)
    move_out = rows_to_tokens(p, sems, block_rows, block_out)
    move_grad = rows_to_tokens(p, sems, grad_rows, input_grad)
    arrays = {"qkv": (qkv_g, qkv_s), "out": (out_g, out_s), "up": (up_g, up_s)}
    items, last, finals = {}, [], []
    pool = list(scratch[:-5])
    for name, (grad, shard) in arrays.items():
        half = grad.shape[-1] // 2
        for offset, width, x_first in PIECES[name]:
            bufs, pool = pool[:6], pool[6:]

            def at(core, grad=grad, half=half, offset=offset, width=width):
                return grad.at[:, :, :, :, pl.ds(core * half + offset, width)]

            items[name, offset] = Scatter(p, sems, at, bufs, not x_first)
            final = bufs[5]
            rows = final.shape[0] // 2
            spot = shard.at[:, pl.ds(p.c * half + offset, width)]
            last += [
                sems.here(final.at[pl.ds(p.c * rows, rows)], spot),
                sems.remote(final.at[pl.ds((1 - p.c) * rows, rows)], spot, p.core),
            ]
            finals.append(final)
    for name, grad, shard in (("vec", vec_g, vec_s), ("down", down_g, down_s)):
        bufs, pool = pool[:6], pool[6:]
        items[name] = Scatter(p, sems, lambda core, grad=grad: grad.at[:, :, :, core], bufs, name == "vec")
        last.append(sems.here(bufs[5], shard))
        finals.append(bufs[5])
    order = ["down", ("up", 0), ("up", 768), ("out", 0), ("qkv", 0), ("qkv", 640), "vec"]
    for t, step in enumerate(scatter_pipeline([items[key] for key in order])):
        step()
        if t == 0:
            begin(move_out)
        if t == 2:
            begin(move_grad)
    begin(last)
    part = jnp.zeros((1, 1), F32)
    for final in finals:
        value = final[...]
        part = part + jnp.sum(jnp.sum(value * value, axis=0, keepdims=True), axis=1, keepdims=True)
    near_sum[p.sq] = jnp.broadcast_to(part, near_sum.shape[1:])
    spread = [
        sems.remote(near_sum.at[p.sq], near_sum.at[p.sq], (p.dp, (p.sq + k) % p.nsq)) for k in range(1, p.nsq)
    ]
    begin(spread)
    finish(spread)
    part = near_sum[0]
    for k in range(1, p.nsq):
        part = part + near_sum[k]
    far_sum[p.dp] = part
    spread = [
        sems.remote(far_sum.at[p.dp], far_sum.at[p.dp], ((p.dp + k) % p.ndp, p.sq)) for k in range(1, p.ndp)
    ]
    begin(spread)
    finish(spread)
    part = far_sum[0]
    for k in range(1, p.ndp):
        part = part + far_sum[k]
    norm[...] = jnp.sqrt(part)
    finish(last + move_out + move_grad)


def scatter_grads(block_rows, grad_rows, qkv_g, out_g, up_g, down_g, vec_g):
    ndp, nsq = lax.axis_size("dp"), lax.axis_size("seq")
    nz = ndp // 2
    part, full, width = block_rows.shape
    token_shape = (part * nsq, full // nsq, width)
    any_space = pl.BlockSpec(memory_space=pl.ANY)
    grid = (nz, 2, nsq // 2)
    rows = D // (ndp * nsq)
    low = FF // (ndp * nsq)
    vec_block = vec_g.shape[-2:]
    shapes = [jax.ShapeDtypeStruct(token_shape, BF16)] * 2
    shapes += [jax.ShapeDtypeStruct((rows, g.shape[1]), F32) for g in (qkv_g, out_g, up_g)]
    shapes += [
        jax.ShapeDtypeStruct((low, D), F32),
        jax.ShapeDtypeStruct(vec_block, F32),
        jax.ShapeDtypeStruct((8, 128), F32),
    ]
    scratch = []
    for name in ("qkv", "out", "up"):
        for _, piece, _ in PIECES[name]:
            scratch += scatter_scratch((2 * rows, piece), nz, BF16)
    scratch += scatter_scratch(vec_block, nz, F32)
    scratch += scatter_scratch((low, D), nz, BF16)
    scratch += [pltpu.SemaphoreType.DMA((80,)), pltpu.SemaphoreType.DMA((80,)), pltpu.SemaphoreType.DMA((24,))]
    scratch += [pltpu.VMEM((nsq, 8, 128), F32), pltpu.VMEM((ndp, 8, 128), F32)]
    return pl.pallas_call(
        scatter_kernel,
        out_shape=shapes,
        in_specs=[any_space] * 7,
        out_specs=[any_space] * 7 + [pl.BlockSpec(memory_space=pltpu.VMEM)],
        scratch_shapes=scratch,
        compiler_params=pltpu.CompilerParams(
            collective_id=2, has_side_effects=True, vmem_limit_bytes=VMEM_LIMIT
        ),
    )(
        block_rows,
        grad_rows,
        qkv_g.reshape(grid + (2 * rows, qkv_g.shape[1])),
        out_g.reshape(grid + (2 * rows, out_g.shape[1])),
        up_g.reshape(grid + (2 * rows, up_g.shape[1])),
        down_g.reshape(grid + (2, low, D)),
        vec_g.reshape(grid + (2,) + vec_block),
    )


def pad_vec(vector, count):
    size = vector.shape[0] // count
    wide = 96 if size % 96 == 0 else size
    parts = vector.astype(F32).reshape(count, size // wide, wide)
    return jnp.pad(parts, ((0, 0), (0, 8 - size // wide), (0, 128 - wide)))


def unpad_vec(parts, size):
    wide = 96 if size % 96 == 0 else size
    return parts[:, : size // wide, :wide].reshape(-1)


def unpack(vector):
    return (
        vector[:D],
        vector[D : 2 * D],
        vector[2 * D : 3 * D],
        vector[3 * D : 4 * D],
        vector[4 * D : 5 * D],
        vector[5 * D : 5 * D + FF],
        vector[5 * D + FF : 6 * D + FF],
        vector[6 * D + FF : 7 * D + FF],
        vector[7 * D + FF : 8 * D + FF],
    )


def normalize(hidden, gain_vec, shift_vec):
    centre = hidden - jnp.mean(hidden, axis=-1, keepdims=True)
    inverse = lax.rsqrt(jnp.mean(centre * centre, axis=-1, keepdims=True) + NORM_EPS)
    normed = centre * inverse
    return (normed * gain_vec + shift_vec, normed, inverse)


def normalize_back(grad_out, normed, inverse, gain_vec):
    scaled = grad_out * gain_vec
    centred = scaled - jnp.mean(scaled, axis=-1, keepdims=True)
    return inverse * (centred - normed * jnp.mean(scaled * normed, axis=-1, keepdims=True))


def gelu_exact(values):
    return jax.nn.gelu(values, approximate=False)


def split_parts(packed_rows):
    full_len = packed_rows.shape[0]
    group_count = packed_rows.shape[-1] // (3 * HEAD_DIM)
    parts = packed_rows.reshape(full_len, 3, group_count, HEAD_DIM)
    return (parts[:, 0], parts[:, 1], parts[:, 2])


def row_probs(queries, key_rows, key_mask):
    scale = 1.0 / math.sqrt(HEAD_DIM)
    scores = jnp.einsum("qhd,khd->hqk", queries, key_rows, preferred_element_type=F32) * scale
    scores = jnp.where(key_mask[None, None, :], scores, MASK_FILL)
    row_peak = jnp.max(scores, axis=-1, keepdims=True)
    row_exp = jnp.exp(scores - row_peak)
    return row_exp / jnp.sum(row_exp, axis=-1, keepdims=True)


def attend_row(packed):
    packed_rows, key_mask = packed
    queries, key_rows, value_rows = split_parts(packed_rows)
    attn_probs = row_probs(queries, key_rows, key_mask)
    mixed_rows = jnp.einsum("hqk,khd->qhd", attn_probs.astype(BF16), value_rows, preferred_element_type=F32)
    return mixed_rows.astype(BF16).reshape(packed_rows.shape[0], D)


def attend_back(packed):
    packed_rows, grad_rows, key_mask = packed
    full_len = packed_rows.shape[0]
    queries, key_rows, value_rows = split_parts(packed_rows)
    grad_mixed = grad_rows.reshape(full_len, HEADS, HEAD_DIM)
    attn_probs = row_probs(queries, key_rows, key_mask)
    grad_probs = jnp.einsum("qhd,khd->hqk", grad_mixed, value_rows, preferred_element_type=F32)
    row_delta = jnp.sum(attn_probs * grad_probs, axis=-1, keepdims=True)
    grad_scores = (attn_probs * (grad_probs - row_delta)).astype(BF16)
    scale = 1.0 / math.sqrt(HEAD_DIM)
    grad_query = jnp.einsum("hqk,khd->qhd", grad_scores, key_rows, preferred_element_type=F32) * scale
    grad_key = jnp.einsum("hqk,qhd->khd", grad_scores, queries, preferred_element_type=F32) * scale
    grad_value = jnp.einsum("hqk,qhd->khd", attn_probs.astype(BF16), grad_mixed, preferred_element_type=F32)
    stacked = jnp.stack([grad_query, grad_key, grad_value], axis=1).astype(BF16)
    return stacked.reshape(full_len, 3 * D)


def adam_step(master, gradient, moment_one, second, factor, decay_rate, step_rate):
    clipped = gradient * factor
    first_new = BETA_ONE * moment_one + (1.0 - BETA_ONE) * clipped
    second_new = BETA_TWO * second + (1.0 - BETA_TWO) * clipped * clipped
    first_hat = first_new / (1.0 - BETA_ONE**STEP_COUNT)
    second_hat = second_new / (1.0 - BETA_TWO**STEP_COUNT)
    updated = master - step_rate * (first_hat / (jnp.sqrt(second_hat) + ADAM_EPS) + decay_rate * master)
    return (updated, first_new, second_new, updated.astype(BF16))


def layer(rows_in, cot_in, token_weight, lengths, qkv_w, out_w, up_w, down_w, vec_w):
    row_count, full_len, width_d = rows_in.shape
    token_count = row_count * full_len
    bias_q, bias_v, bias_o, gain_one, shift_one, bias_up, bias_down, gain_two, shift_two = unpack(vec_w)
    key_mask = jnp.arange(full_len, dtype=jnp.int32)[None, :] < lengths[:, None]
    flat = rows_in.reshape(token_count, width_d)
    merged = jnp.dot(flat, qkv_w, preferred_element_type=F32)
    merged = (merged + jnp.concatenate([bias_q, jnp.zeros_like(bias_q), bias_v])).astype(BF16)
    merged_rows = merged.reshape(row_count, full_len, 3 * width_d)
    mixed = lax.map(attend_row, (merged_rows, key_mask)).reshape(token_count, width_d)
    attn_out = jnp.dot(mixed, out_w, preferred_element_type=F32) + bias_o
    first_out, normed_one, inverse_one = normalize(flat.astype(F32) + attn_out, gain_one, shift_one)
    first_low = first_out.astype(BF16)
    pre_act = jnp.dot(first_low, up_w, preferred_element_type=F32) + bias_up
    activated, gelu_pull = jax.vjp(gelu_exact, pre_act)
    act_low = activated.astype(BF16)
    branch = jnp.dot(act_low, down_w, preferred_element_type=F32) + bias_down
    result, normed_two, inverse_two = normalize(first_out + branch, gain_two, shift_two)
    block_out = result.astype(BF16).reshape(row_count, full_len, width_d)
    grad_result = cot_in.astype(F32) * (token_weight * key_mask.astype(F32))[:, :, None]
    grad_result = grad_result.reshape(token_count, width_d)
    grad_gain_two = jnp.sum(grad_result * normed_two, axis=0)
    grad_shift_two = jnp.sum(grad_result, axis=0)
    grad_second = normalize_back(grad_result, normed_two, inverse_two, gain_two)
    grad_branch = grad_second.astype(BF16)
    grad_bias_down = jnp.sum(grad_branch, axis=0, dtype=F32)
    grad_down = jnp.einsum("tf,td->fd", act_low, grad_branch, preferred_element_type=F32)
    grad_act = jnp.einsum("td,fd->tf", grad_branch, down_w, preferred_element_type=F32)
    grad_pre = gelu_pull(grad_act)[0].astype(BF16)
    grad_bias_up = jnp.sum(grad_pre, axis=0, dtype=F32)
    grad_up = jnp.einsum("td,tf->df", first_low, grad_pre, preferred_element_type=F32)
    grad_first = grad_second + jnp.einsum("tf,df->td", grad_pre, up_w, preferred_element_type=F32)
    grad_gain_one = jnp.sum(grad_first * normed_one, axis=0)
    grad_shift_one = jnp.sum(grad_first, axis=0)
    grad_resid = normalize_back(grad_first, normed_one, inverse_one, gain_one)
    grad_attn = grad_resid.astype(BF16)
    grad_bias_o = jnp.sum(grad_attn, axis=0, dtype=F32)
    grad_out = jnp.einsum("td,te->de", mixed, grad_attn, preferred_element_type=F32)
    grad_mixed = jnp.einsum("te,de->td", grad_attn, out_w, preferred_element_type=F32).astype(BF16)
    grad_merged = lax.map(
        attend_back, (merged_rows, grad_mixed.reshape(row_count, full_len, width_d), key_mask)
    ).reshape(token_count, 3 * width_d)
    grad_qkv = jnp.einsum("td,te->de", flat, grad_merged, preferred_element_type=F32)
    column_sums = jnp.sum(grad_merged, axis=0, dtype=F32)
    input_grad = grad_resid + jnp.einsum("te,de->td", grad_merged, qkv_w, preferred_element_type=F32)
    input_grad = input_grad.astype(BF16).reshape(row_count, full_len, width_d)
    grad_vec = jnp.concatenate(
        [
            column_sums[:width_d],
            column_sums[2 * width_d :],
            grad_bias_o,
            grad_gain_one,
            grad_shift_one,
            grad_bias_up,
            grad_bias_down,
            grad_gain_two,
            grad_shift_two,
        ]
    )
    low = [g.astype(BF16) for g in (grad_qkv, grad_out, grad_up, grad_down)]
    return block_out, input_grad, *low, grad_vec


def body(
    tokens, cotangent, token_weight, lengths,
    qkv_master, out_master, up_master, down_master, vec_master,
    qkv_first, out_first, up_first, down_first, vec_first,
    qkv_second, out_second, up_second, down_second, vec_second,
):
    ndp, nsq = lax.axis_size("dp"), lax.axis_size("seq")
    devices = ndp * nsq
    row_count, local_len, width_d = tokens.shape
    full_len, part = local_len * nsq, row_count // nsq
    vec_size = vec_master.shape[0]
    sq = lax.axis_index("seq")
    my_lengths = lax.dynamic_slice_in_dim(lengths, sq * part, part)
    both = ("dp", "seq")
    own_kernels = qkv_master.shape[0] % 8 == 0 and down_master.shape[0] % 16 == 0 and nsq == 4 and ndp % 2 == 0
    low_vec = vec_master.astype(BF16)
    if own_kernels:
        rows_in, cot_in, weights, qkv_w, out_w, up_w, down_w, vec_w = gather_weights(
            tokens, cotangent, token_weight, qkv_master, out_master, up_master, down_master,
            pad_vec(low_vec, 1)[0],
        )
        qkv_w, out_w, up_w = (w.reshape(-1, w.shape[-1]) for w in (qkv_w, out_w, up_w))
        down_w = down_w.reshape(-1, down_w.shape[-1])
        vec_w = unpad_vec(vec_w.reshape(devices, 8, 128), vec_size)
    else:
        rows_in, cot_in = (
            lax.all_to_all(a, "seq", split_axis=0, concat_axis=1, tiled=True) for a in (tokens, cotangent)
        )
        weights = lax.all_gather(token_weight, "seq", axis=0)
        qkv_w, out_w, up_w, down_w = (
            lax.all_gather(m.astype(BF16), both, axis=0, tiled=True)
            for m in (qkv_master, out_master, up_master, down_master)
        )
        vec_w = lax.all_gather(low_vec, both, axis=0, tiled=True).astype(F32)
    my_weight = lax.dynamic_slice_in_dim(weights, sq * part, part, axis=1)
    my_weight = my_weight.transpose(1, 0, 2).reshape(part, full_len)
    block_rows, grad_rows, *grads, grad_vec = layer(
        rows_in, cot_in, my_weight, my_lengths, qkv_w, out_w, up_w, down_w, vec_w
    )
    if own_kernels:
        block_out, input_grad, *shards, vec_s, norm = scatter_grads(
            block_rows, grad_rows, *grads, pad_vec(grad_vec, devices)
        )
        shards.append(unpad_vec(vec_s[None], vec_size))
        norm_value = norm[0, 0]
    else:
        block_out, input_grad = (
            lax.all_to_all(a, "seq", split_axis=1, concat_axis=0, tiled=True) for a in (block_rows, grad_rows)
        )
        shards = [lax.psum_scatter(g.astype(F32), both, scatter_dimension=0, tiled=True) for g in grads]
        shards.append(lax.psum_scatter(grad_vec, both, scatter_dimension=0, tiled=True))
        norm_value = jnp.sqrt(lax.psum(sum(jnp.sum(s * s) for s in shards), both))
    factor = CLIP_NORM / jnp.maximum(norm_value, CLIP_NORM)
    outs = [block_out, input_grad, norm_value]
    for master, shard, first, second, decay, rate in (
        (qkv_master, shards[0], qkv_first, qkv_second, WEIGHT_DECAY, LEARN_RATE),
        (out_master, shards[1], out_first, out_second, WEIGHT_DECAY, LEARN_RATE),
        (up_master, shards[2], up_first, up_second, WEIGHT_DECAY, LEARN_RATE),
        (down_master, shards[3], down_first, down_second, WEIGHT_DECAY, LEARN_RATE),
        (vec_master, shards[4], vec_first, vec_second, 0.0, VEC_RATE),
    ):
        outs += adam_step(master, shard, first, second, factor, decay, rate)
    return tuple(outs)


def solution(mesh):
    tokens, both, flat = P("dp", "seq", None), P(("dp", "seq"), None), P(("dp", "seq"))
    weights = (both, both, both, both, flat)
    in_specs = (tokens, tokens, P("dp", "seq"), P("dp")) + 3 * weights
    out_specs = (tokens, tokens, P()) + 4 * (both,) * 4 + (flat,) * 4
    return jax.shard_map(body, mesh=mesh, in_specs=in_specs, out_specs=out_specs, check_vma=False)
```

time: 960 us -> 588 us (0.61)
  waiting for transfers between devices: 306 us -> 0 us
  Pallas kernels: 0 us -> 303 us
  blocking collectives: 220 us -> 0 us
  local copies, waits for them, and re-layouts: 129 us -> 41.7 us
  matrix products: 215 us -> 192 us
  between operations: 20.1 us -> 2.41 us
  starting transfers between devices: 14.2 us -> 0 us
    pallas_call x0 -> x2, Pallas kernels: none -> 303 us  [the longest x1 155 us: gather_weights(): pl.pallas_call(gather_kernel, out_shape=shapes, in_specs=[any_space] * 8,...]
    reduce_scatter x4 -> x0, waiting for transfers between devices: 198 us -> none  [the longest x1 123 us: body(): lax.psum_scatter(grad_qkv, ('dp', 'seq'), scatter_dimension=0, tiled=True)]
    all_to_all x1 -> x0, blocking collectives: 98.5 us -> none  [body(): lax.all_to_all(grad_block, 'seq', split_axis=1, concat_axis=3, tiled=True)]
    all_to_all x3 -> x0, waiting for transfers between devices: 85.7 us -> none  [the longest x1 55.1 us: body(): lax.all_to_all(project_heads(), 'seq', split_axis=3, concat_axis=1, tiled...]
    unnamed x2 -> x0, blocking collectives: 81.5 us -> none
    psum x1 -> x0, blocking collectives: 40.2 us -> none  [body(): total_sq = lax.psum(squares, ('dp', 'seq'))]
    all_to_all x7 -> x0, local copies, waits for them, and re-layouts: 38.4 us -> none  [the longest x2 16.3 us: body(): lax.all_to_all(project_heads(), 'seq', split_axis=3, concat_axis=1, tiled...]
    dynamic_slice x40 -> x13, local copies, waits for them, and re-layouts: 32.3 us -> 8.76 us  [the longest x8 7.37 us: layer(): lax.map(attend_row, (merged_rows, key_mask)).reshape(token_count, width_d)]
  transfers between devices with their start and end apart: 11 -> 0, of which waited for: 6 -> 0; matrix products, arithmetic and copies ran while one was open for 29% -> 0% of each run, Pallas kernels for 0% -> 0%
where the time goes in v1:
time: 588 us; the launch traced here: 580 us
  Pallas kernels  303 us (52%)
  matrix products  192 us (33%)
  local copies, waits for them, and re-layouts  41.7 us (7%)
  other arithmetic  40.1 us (7%)
    pallas_call x1, Pallas kernels, gather_weights(): pl.pallas_call(gather_kernel, out_shape=shapes, in_specs=[any_space] * 8,...  155 us
    pallas_call x1, Pallas kernels, scatter_grads(): pl.pallas_call(scatter_kernel, out_shape=shapes, in_specs=[any_space] * 7...  148 us
    dot_general x1, matrix products, layer(): pre_act = jnp.dot(first_low, up_w, preferred_element_type=F32) + bias_up  37.9 us
    sub x4, matrix products, row_probs(): row_exp = jnp.exp(scores - row_peak)  29.9 us
    dot_general x1, matrix products, layer(): jnp.einsum('td,fd->tf', grad_branch, down_w, preferred_element_type=F32)  19.2 us
    dot_general x2, matrix products, attend_back(): jnp.einsum('hqk,qhd->khd', attn_probs.astype(BF16), grad_mixed, preferred...  13.5 us
    convert_element_type x2, other arithmetic, attend_back(): grad_scores = (attn_probs * (grad_probs - row_delta)).astype(BF16)  13.4 us

profile of v1, /device:TPU:0, one launch (start us, length us, event | category | flops | bytes accessed | tf_op | source)
XLA Modules:
  0.0 580.0 jit_solution(7019274636039060102)
XLA Ops:
  2.8 154.9 %shard_map.362 = (bf16[2,512,768]{2,1,0:T(8,128)(2,1)}, bf16[2,512,768]{2,1,0:T(8,128)(2,1)}, f32[4,8,128]{2,1,0:T(8,128)}, bf16[4,2,2,48,2304]{4,3,2,1,0:T(8,12...) custom-call(bf16[8,128,768]{2,1,0:T(8,128)(2,1)} %tokens.1, ...), custom_call_target="tpu_custom_call" | custom-call | tf_op jit(solution)/shard_map/pallas_call | solution.py:230
  160.5 4.2 fusion.41
  165.3 5.5 add_convert_fusion.1
  170.8 6.6 %copy.55 = bf16[2,512,2304]{1,2,0:T(8,128)(2,1)} copy(bf16[2,512,2304]{2,1,0:T(8,128)(2,1)} %bitcast.189) | data formatting | bytes 9437184 | tf_op jit(solution)/shard_map/while | solution.py:550
  177.4 32.7 %while.20 = (s32[]{:T(128)}, bf16[2,512,768]{2,1,0:T(8,128)(2,1)}, bf16[2,512,2304]{1,2,0:T(8,128)(2,1)}, pred[2,512]{1,0:T(4,128)(4,1)S(1)}, s32[]{:T(128)}) while((s32[]{:T(128)}, bf16[2,512,768]{2,1,0:T(8,128)(2,1)}, bf16[2,512,2304]{1,2,0:T(8,128)(2,1)}, pred[2,512]{1,0:T(4,128)(4,1)S(1)}, s32[]{:T(128)}) %tuple.86), condition=%wide.region_3.4_spmd, body=%wide.region_0.3_spmd.sunk | while | flops 824574464 | bytes 36234832 | solution.py:550
  177.4 1.8 constant_dynamic-slice_fusion.6
  179.3 7.5 %fusion.103 = (f32[12,512]{1,0:T(8,128)S(1)}, f32[12,512,512]{1,2,0:T(8,128)}) fusion(pred[512]{0:T(512)(128)(4,1)S(1)} %dynamic-slice_reduce_fusion.4, bf16[512,3,12,64]{0,3,2,1:T(8,128)(2,1)S(1)} %bitcast.181), kind=kOutput, calls=%fused_computation.153.clone.1 | convolution fusion | flops 415236608 | bytes 14180864 | tf_op jit(solution)/shard_map/while/body/eval_jaxpr/sub | solution.py:502
  186.7 5.8 fusion.104
  193.8 1.8 constant_dynamic-slice_fusion.6
  195.6 7.5 %fusion.103 = (f32[12,512]{1,0:T(8,128)S(1)}, f32[12,512,512]{1,2,0:T(8,128)}) fusion(pred[512]{0:T(512)(128)(4,1)S(1)} %dynamic-slice_reduce_fusion.4, bf16[512,3,12,64]{0,3,2,1:T(8,128)(2,1)S(1)} %bitcast.181), kind=kOutput, calls=%fused_computation.153.clone.1 | convolution fusion | flops 415236608 | bytes 14180864 | tf_op jit(solution)/shard_map/while/body/eval_jaxpr/sub | solution.py:502
  203.1 5.8 fusion.104
  210.1 3.9 fusion.68
  214.6 37.9 %multiply_convert_fusion.3 = (bf16[1024,3072]{1,0:T(8,128)(2,1)S(1)}, f32[1024,3072]{1,0:T(8,128)}, f32[1024,3072]{1,0:T(8,128)}) fusion(f32[3072]{0:T(1024)S(1)} %slice.86, bf16[768,3072]{1,0:T(8,128)(2,1)} %bitcast.199, f32[1024,768]{1,0:T(8,128)S(1)} %get-tuple-element.193, f32[768]{0:T(1024)S(1)} %get-tuple-element.187, ...), kind=kOutput, calls=%fused_computation.55 | convolution fusion | flops 5043388416 | bytes 39348224 | tf_op jit(solution)/shard_map/dot_general | solution.py:554
  252.5 5.5 fusion.69
  259.9 1.6 fusion.39
  261.5 3.7 convert_reduce_fusion.2
  265.2 19.2 %convert_reduce_fusion = (f32[3072]{0:T(1024)}, bf16[1024,3072]{1,0:T(8,128)(2,1)}) fusion(f32[1024,3072]{1,0:T(8,128)} %get-tuple-element.175, bf16[3072,768]{1,0:T(8,128)(2,1)} %bitcast.201, f32[1024,768]{1,0:T(8,128)} %get-tuple-element.171, f32[1024,3072]{1,0:T(8,128)} %get-tuple-element.194, f32[3072]{0:T(1024)S(1)} %slice.86), kind=kOutput, calls=%fused_computation.53 | convolution fusion | flops 4886098944 | bytes 39346176 | tf_op jit(solution)/shard_map/td,fd->tf/dot_general | solution.py:568
  284.5 10.4 %convolution_convert_fusion = bf16[3072,768]{1,0:T(8,128)(2,1)} fusion(bf16[1024,3072]{1,0:T(8,128)(2,1)} %copy-done.44, f32[1024,768]{1,0:T(8,128)} %get-tuple-element.171), kind=kOutput, calls=%fused_computation.72 | convolution fusion | flops 4834983936 | bytes 14155776 | tf_op jit(solution)/shard_map/tf,td->fd/dot_general | solution.py:567
  294.8 9.1 %multiply_reduce_fusion.1 = (f32[768]{0:T(1024)}, f32[1024]{0:T(1024)S(1)}, f32[1024]{0:T(1024)S(1)}, f32[768]{0:T(1024)}, f32[1024,768]{1,0:T(8,128)S(1)}) fusion(f32[1024,768]{1,0:T(8,128)S(1)} %get-tuple-element.193, f32[1024]{0:T(1024)S(1)} %add_rsqrt_fusion.1, f32[1024]{0:T(1024)S(1)} %broadcast_multiply_fusion.4, f32[768]{0:T(1024)S(1)} %get-tuple-element.188, ...), kind=kOutput, calls=%fused_computation.78 | convolution fusion | flops 4839698432 | bytes 20472832 | tf_op jit(solution)/shard_map/tf,df->td/dot_general | solution.py:572
  303.9 1.7 convert_reduce_fusion.3
  305.6 8.1 %convolution_convert_fusion.1 = bf16[768,3072]{1,0:T(8,128)(2,1)} fusion(bf16[1024,3072]{1,0:T(8,128)(2,1)S(1)} %copy-done.43, f32[1024,768]{1,0:T(8,128)S(1)} %get-tuple-element.193, f32[768]{0:T(1024)S(1)} %get-tuple-element.187, f32[768]{0:T(1024)S(1)} %get-tuple-element.188, f32[1024]{0:T(1024)S(1)} %add_rsqrt_fusion.1, ...), kind=kOutput, calls=%fused_computation.73 | convolution fusion | flops 4838129664 | bytes 14170112 | tf_op jit(solution)/shard_map/td,tf->df/dot_general | solution.py:571
  313.8 2.5 convolution_convert_fusion.3
  316.3 1.5 convolution_convert_fusion.2
  317.8 73.1 %while.21 = (s32[]{:T(128)}, bf16[2,512,2304]{1,2,0:T(8,128)(2,1)}, bf16[2,512,2304]{1,2,0:T(8,128)(2,1)}, pred[2,512]{1,0:T(4,128)(4,1)S(1)}, bf16[2,512,768]{2,1,0:T(8,128)(2,1)S(1)}, /*index=5*/s32[]{:T(128)}) while((s32[]{:T(128)}, bf16[2,512,2304]{1,2,0:T(8,128)(2,1)}, bf16[2,512,2304]{1,2,0:T(8,128)(2,1)}, ...), condition=%wide.region_16.17_spmd, body=%wide.region_12.16_spmd.sunk | while | flops 2058480128 | bytes 182609600 | solution.py:580
  318.9 1.8 constant_dynamic-slice_fusion.8
  320.7 7.5 %fusion.110 = (f32[12,512]{1,0:T(8,128)S(1)}, f32[12,512,512]{1,2,0:T(8,128)}) fusion(pred[512]{0:T(512)(128)(4,1)S(1)} %dynamic-slice_reduce_fusion.5, bf16[512,3,12,64]{0,3,2,1:T(8,128)(2,1)S(1)} %bitcast.177), kind=kOutput, calls=%fused_computation.154.clone.1 | convolution fusion | flops 415236608 | bytes 14180864 | tf_op jit(solution)/shard_map/while/body/eval_jaxpr/sub | solution.py:502
  328.2 6.8 %fusion.111 = bf16[512,1,12,64]{0,3,2,1:T(8,128)(2,1)S(1)} fusion(bf16[512,12,64]{0,2,1:T(8,128)(2,1)S(1)} %bitcast.183, f32[12,512,512]{1,2,0:T(8,128)} %get-tuple-element.266, f32[12,512]{1,0:T(8,128)S(1)} %get-tuple-element.267), kind=kOutput, calls=%fused_computation.37.clone.1 | convolution fusion | flops 409337856 | bytes 14180352 | tf_op jit(solution)/shard_map/while/body/eval_jaxpr/hqk,qhd->khd/dot_general | solution.py:526
  335.0 1.4 copy-done
  336.4 5.6 multiply_reduce_fusion.9
  341.9 6.7 %multiply_convert_fusion.5 = bf16[12,512,512]{1,2,0:T(8,128)(2,1)S(1)} fusion(f32[12,512,512]{1,2,0:T(8,128)} %get-tuple-element.268, f32[12,512]{1,0:T(8,128)S(1)} %get-tuple-element.269, f32[12,512,512]{1,2,0:T(8,128)S(1)} %copy-done, f32[12,512]{1,0:T(8,128)S(1)} %get-tuple-element.267), kind=kLoop, calls=%fused_computation.21.clone.1 | loop fusion | flops 12582912 | bytes 31506432 | tf_op jit(solution)/shard_map/while/body/eval_jaxpr/convert_element_type | solution.py:522
  349.8 2.0 fusion.112
  352.1 1.5 constant_dynamic-update-slice_fusion.12
  355.3 1.8 constant_dynamic-slice_fusion.8
  357.2 7.5 %fusion.110 = (f32[12,512]{1,0:T(8,128)S(1)}, f32[12,512,512]{1,2,0:T(8,128)}) fusion(pred[512]{0:T(512)(128)(4,1)S(1)} %dynamic-slice_reduce_fusion.5, bf16[512,3,12,64]{0,3,2,1:T(8,128)(2,1)S(1)} %bitcast.177), kind=kOutput, calls=%fused_computation.154.clone.1 | convolution fusion | flops 415236608 | bytes 14180864 | tf_op jit(solution)/shard_map/while/body/eval_jaxpr/sub | solution.py:502
  364.6 6.8 %fusion.111 = bf16[512,1,12,64]{0,3,2,1:T(8,128)(2,1)S(1)} fusion(bf16[512,12,64]{0,2,1:T(8,128)(2,1)S(1)} %bitcast.183, f32[12,512,512]{1,2,0:T(8,128)} %get-tuple-element.266, f32[12,512]{1,0:T(8,128)S(1)} %get-tuple-element.267), kind=kOutput, calls=%fused_computation.37.clone.1 | convolution fusion | flops 409337856 | bytes 14180352 | tf_op jit(solution)/shard_map/while/body/eval_jaxpr/hqk,qhd->khd/dot_general | solution.py:526
  371.4 1.4 copy-done
  372.8 5.6 multiply_reduce_fusion.9
  378.4 6.7 %multiply_convert_fusion.5 = bf16[12,512,512]{1,2,0:T(8,128)(2,1)S(1)} fusion(f32[12,512,512]{1,2,0:T(8,128)} %get-tuple-element.268, f32[12,512]{1,0:T(8,128)S(1)} %get-tuple-element.269, f32[12,512,512]{1,2,0:T(8,128)S(1)} %copy-done, f32[12,512]{1,0:T(8,128)S(1)} %get-tuple-element.267), kind=kLoop, calls=%fused_computation.21.clone.1 | loop fusion | flops 12582912 | bytes 31506432 | tf_op jit(solution)/shard_map/while/body/eval_jaxpr/convert_element_type | solution.py:522
  386.2 2.0 fusion.112
  388.5 1.6 constant_dynamic-update-slice_fusion.12
  391.0 3.1 convert_reduce_fusion.1
  395.1 7.8 %bitcast_convert_fusion = bf16[768,2304]{1,0:T(8,128)(2,1)} fusion(bf16[2,512,768]{2,1,0:T(8,128)(2,1)S(1)} %copy-done.40, bf16[2,512,2304]{1,2,0:T(8,128)(2,1)} %get-tuple-element.97), kind=kOutput, calls=%fused_computation.71 | convolution fusion | flops 3625648128 | bytes 9830400 | tf_op jit(solution)/shard_map/td,te->de/dot_general | solution.py:583
  402.9 6.8 %copy.59 = bf16[2,512,2304]{2,1,0:T(8,128)(2,1)} copy(bf16[2,512,2304]{1,2,0:T(8,128)(2,1)} %get-tuple-element.97) | data formatting | bytes 9437184 | tf_op jit(solution)/shard_map/while | solution.py:580
  409.7 8.4 %add_convert_fusion.2 = bf16[1024,768]{1,0:T(8,128)(2,1)} fusion(f32[1024,768]{1,0:T(8,128)S(1)} %copy-done.5, bf16[1024,2304]{1,0:T(8,128)(2,1)} %bitcast.188, bf16[768,2304]{1,0:T(8,128)(2,1)} %bitcast.205), kind=kOutput, calls=%fused_computation.80 | convolution fusion | flops 3625451520 | bytes 12976128 | tf_op jit(solution)/shard_map/te,de->td/dot_general | solution.py:585
  418.2 148.5 %shard_map.363 = (bf16[8,128,768]{2,1,0:T(8,128)(2,1)}, bf16[8,128,768]{2,1,0:T(8,128)(2,1)}, f32[24,2304]{1,0:T(8,128)}, f32[24,768]{1,0:T(8,128)}, f32[24,3072...) custom-call(bf16[2,512,768]{2,1,0:T(8,128)(2,1)} %bitcast.187, ...), custom_call_target="tpu_custom_call" | custom-call | tf_op jit(solution)/shard_map/pallas_call | solution.py:427
  570.2 1.6 fusion.60
  571.8 2.1 fusion.62
  573.9 2.2 fusion.56
  (158 shorter events, 23.6 us)
Async XLA Ops:
  157.7 7.6 %copy-start.39 = (bf16[2,512,768]{2,1,0:T(8,128)(2,1)S(1)}, bf16[2,512,768]{2,1,0:T(8,128)(2,1)}, u32[]{:S(2)}) copy-start(bf16[2,512,768]{2,1,0:T(8,128)(2,1)} %get-tuple-element.88) | copy-start | bytes 4718596
  158.9 6.4 %copy-start.38 = (bf16[4,2,2,48,2304]{4,3,2,1,0:T(8,128)(2,1)S(1)}, bf16[4,2,2,48,2304]{4,3,2,1,0:T(8,128)(2,1)}, u32[]{:S(2)}) copy-start(bf16[4,2,2,48,2304]{4,3,2,1,0:T(8,128)(2,1)} %get-tuple-element.89) | copy-start | bytes 10616836
  160.5 10.3 %copy-start.22 = (f32[768]{0:T(1024)}, f32[768]{0:T(1024)S(1)}, u32[]{:S(2)}) copy-start(f32[768]{0:T(1024)S(1)} %get-tuple-element.184) | copy-start | bytes 9220
  210.1 3.9 copy-start.18
  210.1 42.4 %slice-start = ((s8[4718592]{0:T(1024)(128)(4,1)}), s8[4194304]{0:T(1024)(128)(4,1)S(1)}, s32[]{:S(2)}) async-start(s8[4718592]{0:T(1024)(128)(4,1)} %bitcast.202), calls=%async_computation | async-start | bytes 8388608
  214.6 37.9 %copy-start.33 = (f32[768]{0:T(1024)S(1)}, f32[768]{0:T(1024)}, u32[]{:S(2)}) copy-start(f32[768]{0:T(1024)} %get-tuple-element.186) | copy-start | bytes 9220
  214.6 37.9 %slice-start.1 = ((s8[4718592]{0:T(1024)(128)(4,1)}), s8[524288]{0:T(1024)(128)(4,1)S(1)}, s32[]{:S(2)}) async-start(s8[4718592]{0:T(1024)(128)(4,1)} %bitcast.202), calls=%async_computation.1 | async-start | bytes 1048576
  252.5 5.5 copy-start.44
  252.5 6.1 %copy-start.23 = (f32[768]{0:T(1024)S(1)}, f32[768]{0:T(1024)}, u32[]{:S(2)}) copy-start(f32[768]{0:T(1024)} %copy-done.22) | copy-start | bytes 9220
  258.0 1.9 copy-start.1
  258.6 3.0 copy-start.25
  258.6 3.0 copy-start.28
  284.5 10.4 %copy-start.6 = (f32[1024,768]{1,0:T(8,128)S(1)}, f32[1024,768]{1,0:T(8,128)}, u32[]{:S(2)}) copy-start(f32[1024,768]{1,0:T(8,128)} %get-tuple-element.171) | copy-start | bytes 9437188
  284.5 10.4 %copy-start.43 = (bf16[1024,3072]{1,0:T(8,128)(2,1)S(1)}, bf16[1024,3072]{1,0:T(8,128)(2,1)}, u32[]{:S(2)}) copy-start(bf16[1024,3072]{1,0:T(8,128)(2,1)} %get-tuple-element.199) | copy-start | bytes 18874372
  305.6 10.7 %copy-start.4 = (f32[1024,768]{1,0:T(8,128)}, f32[1024,768]{1,0:T(8,128)S(1)}, u32[]{:S(2)}) copy-start(f32[1024,768]{1,0:T(8,128)S(1)} %get-tuple-element.173) | copy-start | bytes 9437188
  305.6 8.1 %copy-start.41 = (bf16[2,512,768]{2,1,0:T(8,128)(2,1)S(1)}, bf16[2,512,768]{2,1,0:T(8,128)(2,1)}, u32[]{:S(2)}) copy-start(bf16[2,512,768]{2,1,0:T(8,128)(2,1)} %get-tuple-element.91) | copy-start | bytes 4718596
  313.8 2.5 copy-start.42
  316.3 1.5 copy-start.19
  328.2 8.2 %copy-start = (f32[12,512,512]{1,2,0:T(8,128)S(1)}, f32[12,512,512]{1,2,0:T(8,128)}, u32[]{:S(2)}) copy-start(f32[12,512,512]{1,2,0:T(8,128)} %get-tuple-element.266) | copy-start | bytes 37748740 | tf_op jit(solution)/shard_map/while
  352.1 2.1 copy-start.3
  364.6 8.2 %copy-start = (f32[12,512,512]{1,2,0:T(8,128)S(1)}, f32[12,512,512]{1,2,0:T(8,128)}, u32[]{:S(2)}) copy-start(f32[12,512,512]{1,2,0:T(8,128)} %get-tuple-element.266) | copy-start | bytes 37748740 | tf_op jit(solution)/shard_map/while
  388.5 2.1 copy-start.3
  390.8 3.3 copy-start.24
  390.9 3.3 copy-start.29
  390.9 3.3 copy-start.35
  390.9 3.3 copy-start.34
  390.9 3.3 copy-start.31
  390.9 3.3 copy-start.27
  390.9 3.3 copy-start.30
  390.9 3.3 copy-start.26
  390.9 4.1 copy-start.40
  402.9 6.9 %copy-start.5 = (f32[1024,768]{1,0:T(8,128)S(1)}, f32[1024,768]{1,0:T(8,128)}, u32[]{:S(2)}) copy-start(f32[1024,768]{1,0:T(8,128)} %copy-done.4) | copy-start | bytes 9437188
  418.2 151.4 %copy-start.32 = (f32[288]{0:T(512)S(1)}, f32[288]{0:T(512)}, u32[]{:S(2)}) copy-start(f32[288]{0:T(512)} %param.31) | copy-start | bytes 3460
  418.2 151.4 %copy-start.36 = (f32[288]{0:T(512)S(1)}, f32[288]{0:T(512)}, u32[]{:S(2)}) copy-start(f32[288]{0:T(512)} %param.36) | copy-start | bytes 3460
  418.2 151.4 %copy-start.37 = (f32[288]{0:T(512)S(1)}, f32[288]{0:T(512)}, u32[]{:S(2)}) copy-start(f32[288]{0:T(512)} %param.41) | copy-start | bytes 3460
  418.2 152.0 %copy-start.17 = (f32[24,768]{1,0:T(8,128)S(1)}, f32[24,768]{1,0:T(8,128)}, u32[]{:S(2)}) copy-start(f32[24,768]{1,0:T(8,128)} %out_m.1) | copy-start | bytes 221188
  418.2 152.0 %copy-start.20 = (f32[24,768]{1,0:T(8,128)S(1)}, f32[24,768]{1,0:T(8,128)}, u32[]{:S(2)}) copy-start(f32[24,768]{1,0:T(8,128)} %param.33) | copy-start | bytes 221188
  418.2 152.0 %copy-start.21 = (f32[24,768]{1,0:T(8,128)S(1)}, f32[24,768]{1,0:T(8,128)}, u32[]{:S(2)}) copy-start(f32[24,768]{1,0:T(8,128)} %param.38) | copy-start | bytes 221188
  418.2 153.6 %copy-start.11 = (f32[24,2304]{1,0:T(8,128)S(1)}, f32[24,2304]{1,0:T(8,128)}, u32[]{:S(2)}) copy-start(f32[24,2304]{1,0:T(8,128)} %qkv_m.1) | copy-start | bytes 663556
  418.2 155.7 %copy-start.9 = (f32[96,768]{1,0:T(8,128)S(1)}, f32[96,768]{1,0:T(8,128)}, u32[]{:S(2)}) copy-start(f32[96,768]{1,0:T(8,128)} %down_m.1) | copy-start | bytes 884740
  418.2 155.7 %copy-start.12 = (f32[96,768]{1,0:T(8,128)S(1)}, f32[96,768]{1,0:T(8,128)}, u32[]{:S(2)}) copy-start(f32[96,768]{1,0:T(8,128)} %param.35) | copy-start | bytes 884740
  418.2 155.7 %copy-start.13 = (f32[96,768]{1,0:T(8,128)S(1)}, f32[96,768]{1,0:T(8,128)}, u32[]{:S(2)}) copy-start(f32[96,768]{1,0:T(8,128)} %param.40) | copy-start | bytes 884740
  566.7 9.4 %copy-start.10 = (f32[24,3072]{1,0:T(8,128)S(1)}, f32[24,3072]{1,0:T(8,128)}, u32[]{:S(2)}) copy-start(f32[24,3072]{1,0:T(8,128)} %up_m.1) | copy-start | bytes 884740
  566.7 9.4 %copy-start.14 = (f32[24,3072]{1,0:T(8,128)S(1)}, f32[24,3072]{1,0:T(8,128)}, u32[]{:S(2)}) copy-start(f32[24,3072]{1,0:T(8,128)} %param.34) | copy-start | bytes 884740
  566.7 10.5 %copy-start.8 = (bf16[8,128,768]{2,1,0:T(8,128)(2,1)S(1)}, bf16[8,128,768]{2,1,0:T(8,128)(2,1)}, u32[]{:S(2)}) copy-start(bf16[8,128,768]{2,1,0:T(8,128)(2,1)} %get-tuple-element.326) | copy-start | bytes 4718596
  569.5 6.6 %copy-start.15 = (f32[24,3072]{1,0:T(8,128)S(1)}, f32[24,3072]{1,0:T(8,128)}, u32[]{:S(2)}) copy-start(f32[24,3072]{1,0:T(8,128)} %param.39) | copy-start | bytes 884740
  569.6 6.6 %copy-start.16 = (f32[24,3072]{1,0:T(8,128)S(1)}, f32[24,3072]{1,0:T(8,128)}, u32[]{:S(2)}) copy-start(f32[24,3072]{1,0:T(8,128)} %get-tuple-element.103) | copy-start | bytes 884740
  573.9 4.5 copy-start.7
  (2 other events, 2.3 us)
